TPU v7x, 256 devices: a whole 4x4x8 slice. The times are simulated.
256 devices in a mesh: stn: 64 (over z, y_hi, x), chan: 4 (over y_lo, core).
Axes of the slice: x: 4, y: 4 (y_hi: 2, y_lo: 2; y = y_hi * 2 + y_lo), z: 8, core: 2. Of those that a mesh axis runs over, the one named last changes fastest.
Arguments:
- samples: bfloat16 [512, 17, 2, 8192], P(('stn', 'chan')), may hold values from -6 to 6
- keeper: int32 [64, 64], replicated, may hold values from 0 to 1, as said below
Outputs:
- visibilities: bfloat16 [512, 2, 4096, 264], P('stn', None, 'chan')
Inputs may be any that keep to these rules, and one draw needn't show every extreme that they name: keeper[g, g] is 1; for g != h with d = (g - h) mod 64: keeper[g, h] is 1 where 0 < d < 32, 0 where d > 32, and at d = 32 exactly one of keeper[g, h] and keeper[h, g] is 1, which one drawn for each such pair; half of the rows hold 33 ones, the others 33 - 1.
All inputs are finite; a program needn't handle non-finite values.
Results may differ from a plain program's by a relative error of at most 0.0077.
Values may be sent and summed in bfloat16 or wider, within the bound.
No kernel may reach another device: no remote copies, remote signals or barrier semaphores. Data moves between devices by JAX's collectives and lax.ppermute only.
A program may use at most 192 MiB of HBM per device.

v0:
```python
import math
import jax
import jax.numpy as jnp
from jax import lax
from jax.sharding import PartitionSpec as P

NFFT = 8192
TAPS = 16
CH_WIN = 1024
DFT_BLOCK = 256


def taps_table():
    pos = jnp.arange(TAPS * NFFT).astype(jnp.float32)
    shifted = (pos + 0.5) / NFFT - TAPS / 2.0
    window = 0.5 - 0.5 * jnp.cos(2.0 * math.pi * (pos + 0.5) / (TAPS * NFFT))
    return (jnp.sinc(shifted) * window).reshape(TAPS, NFFT)


def twiddles(width):
    index_n = jnp.arange(NFFT, dtype=jnp.int32)[:, None]
    index_k = jnp.arange(width, dtype=jnp.int32)[None, :]
    phase = (index_n * index_k % NFFT).astype(jnp.float32) * (2.0 * math.pi / NFFT)
    cosines = jnp.cos(phase).astype(jnp.bfloat16)
    sines = jnp.sin(phase).astype(jnp.bfloat16)
    upper = jnp.concatenate([cosines, -sines], axis=1)
    lower = jnp.concatenate([sines, cosines], axis=1)
    return jnp.concatenate([upper, lower], axis=0)


def rotations(ch_tot, width):
    blocks = ch_tot // width
    index_n = jnp.arange(NFFT, dtype=jnp.int32)[None, :]
    index_b = jnp.arange(blocks, dtype=jnp.int32)[:, None]
    phase = (index_n * index_b * width % NFFT).astype(jnp.float32) * (2.0 * math.pi / NFFT)
    return (jnp.cos(phase), jnp.sin(phase))


def channelise(block, taps, table, cos_rot, sin_rot, ch_tot):
    frames = block.shape[1] - TAPS + 1
    count = block.shape[0]
    width = table.shape[1] // 2
    blocks = ch_tot // width
    total = taps[0] * block[:, 0:frames].astype(jnp.float32)
    for tap in range(1, TAPS):
        total = total + taps[tap] * block[:, tap : tap + frames].astype(jnp.float32)
    real_part = total[:, :, 0][None]
    imag_part = total[:, :, 1][None]
    cosine = cos_rot[:, None, None, :]
    sine = sin_rot[:, None, None, :]
    rot_real = real_part * cosine + imag_part * sine
    rot_imag = imag_part * cosine - real_part * sine
    lhs = jnp.stack([rot_real, rot_imag], axis=3).astype(jnp.bfloat16)
    lhs = lhs.reshape(blocks * count * frames, 2 * NFFT)
    spectrum = jnp.dot(lhs, table, preferred_element_type=jnp.float32) * (1.0 / math.sqrt(NFFT))
    spectrum = spectrum.astype(jnp.bfloat16).reshape(blocks, count, frames, 2, width)
    spectrum = jnp.transpose(spectrum, (1, 0, 4, 3, 2))
    return spectrum.reshape(count, ch_tot, 2, frames)


def correlate(own, others, frames):
    half = others.shape[2] // 2
    turned = jnp.concatenate([-others[:, :, half:], others[:, :, :half]], axis=2)
    rhs = jnp.concatenate([others, turned], axis=0)
    product = lax.dot_general(
        own, rhs, (((2,), (2,)), ((1,), (1,))), preferred_element_type=jnp.float32
    )
    rows = others.shape[0]
    product = product.reshape(product.shape[0], product.shape[1], 2, rows)
    return jnp.transpose(product, (1, 2, 0, 3)) / frames


def slot_table(keep_rows, keep_slots):
    ranking = jnp.cumsum(keep_rows, axis=1) - 1
    slot_index = jnp.arange(keep_slots, dtype=jnp.int32)
    matched = (keep_rows[:, :, None] == 1) & (ranking[:, :, None] == slot_index[None, None, :])
    column_ids = jnp.arange(keep_rows.shape[1], dtype=jnp.int32)
    slot_column = jnp.sum(jnp.where(matched, column_ids[None, :, None], 0), axis=1)
    filled = jnp.any(matched, axis=1)
    return (slot_column, filled)


def per_device(samples, keeper):
    n_chan = lax.axis_size("chan")
    n_stn = lax.axis_size("stn")
    ch_tot = CH_WIN * n_chan
    frames = samples.shape[1] - TAPS + 1
    cos_rot, sin_rot = rotations(ch_tot, DFT_BLOCK)
    spectrum = channelise(samples, taps_table(), twiddles(DFT_BLOCK), cos_rot, sin_rot, ch_tot)
    local = lax.all_to_all(spectrum, "chan", split_axis=1, concat_axis=0, tiled=True)
    group_in = local.shape[0]
    own = local.reshape(group_in, CH_WIN, 2 * frames)
    keep_slots = n_stn // 2 + 1
    group_index = lax.axis_index("stn")
    row_keep = jnp.take(keeper, group_index, axis=0)
    slot_column, filled = slot_table(row_keep[None], keep_slots)
    slot_column = slot_column[0]
    filled = filled[0]
    nothing = jnp.zeros((), jnp.bfloat16)
    col_mask = jnp.repeat(row_keep, group_in).astype(jnp.float32)
    tile = correlate(own, lax.all_gather(own, "stn", axis=0, tiled=True), frames)
    whole = (tile * col_mask[None, None, None, :]).astype(jnp.bfloat16)
    whole = whole.reshape(group_in, 2, CH_WIN, n_stn, group_in)
    picked = jnp.take(whole, slot_column, axis=3)
    picked = jnp.where(filled[None, None, None, :, None], picked, nothing)
    return picked.reshape(group_in, 2, CH_WIN, keep_slots * group_in)


def solution(mesh):
    placed = (P(("stn", "chan"), None, None, None), P())
    return jax.shard_map(
        per_device,
        mesh=mesh,
        in_specs=placed,
        out_specs=P("stn", None, "chan", None),
        check_vma=False,
    )
```

profile of v0, /device:TPU:2, one launch (start us, length us, event | category | flops | bytes accessed | tf_op | source)
XLA Modules:
  0.0 386.7 jit_solution(5526646558050877336)
XLA Ops:
  6.5 2.4 fusion.33
  8.9 2.1 fusion.45
  11.0 35.0 %sine_convert_fusion = (bf16[8192,256]{1,0:T(8,128)(2,1)}, bf16[8192,256]{1,0:T(8,128)(2,1)}) fusion(), kind=kLoop, calls=%fused_computation.25 | loop fusion | flops 33554432 | bytes 8388608 | tf_op jit(solution)/shard_map/convert_element_type | solution.py:25
  46.0 32.4 %fusion.22 = bf16[8192,256]{1,0:T(8,128)(2,1)} fusion(), kind=kLoop, calls=%fused_computation.34 | loop fusion | flops 37748736 | bytes 4194304 | tf_op jit(solution)/shard_map/neg | solution.py:26
  78.4 2.1 multiply_add_fusion.1
  81.0 4.4 %add_convert_fusion = (bf16[16,2,2,1,8192]{4,3,2,1,0:T(2,128)(2,1)S(1)}, bf16[16,2,2,1,8192]{4,3,2,1,0:T(2,128)(2,1)S(1)}) fusion(f32[16,8192]{1,0:T(8,128)S(1)} %get-tuple-element.42, f32[2,2,8192]{2,1,0:T(2,128)S(1)} %get-tuple-element.40, f32[16,8192]{1,0:T(8,128)S(1)} %get-tuple-element.43, f32[2,2,8192]{2,1,0:T(2,128)S(1)} %get-tuple-element.41), kind=kLoop, calls=%fused_computation.33 | loop fusion | flops 4194304 | bytes 3407872 | tf_op jit(solution)/shard_map/convert
  85.4 4.8 %pad_maximum_fusion = bf16[16,2,2,2,8192]{4,3,2,1,0:T(2,128)(2,1)S(1)} fusion(bf16[16,2,2,1,8192]{4,3,2,1,0:T(2,128)(2,1)S(1)} %get-tuple-element.21, bf16[16,2,2,1,8192]{4,3,2,1,0:T(2,128)(2,1)S(1)} %get-tuple-element.20), kind=kLoop, calls=%fused_computation.31 | loop fusion | flops 4194304 | bytes 4194304 | tf_op jit(solution)/shard_map/stack | solution.py:53
  90.2 1.2 copy.51
  91.4 13.7 %fusion.26 = bf16[64,512]{1,0:T(8,128)(2,1)S(1)} fusion(bf16[64,16384]{1,0:T(8,128)(2,1)S(1)} %bitcast.44, bf16[8192,256]{1,0:T(8,128)(2,1)} %get-tuple-element.45, bf16[8192,256]{1,0:T(8,128)(2,1)} %get-tuple-element.44, bf16[8192,256]{1,0:T(8,128)(2,1)} %fusion.22), kind=kOutput, calls=%fused_computation.36 | convolution fusion | flops 1140916224 | bytes 14745600 | tf_op jit(solution)/shard_map/dot_general | solution.py:55
  105.2 4.8 %copy.46 = bf16[2,16,256,2,2]{4,3,0,2,1:T(2,128)(2,1)} copy(bf16[2,16,256,2,2]{2,1,4,3,0:T(8,128)(2,1)S(1)} %bitcast.45) | data formatting | bytes 131072 | tf_op jit(solution)/shard_map/reshape | solution.py:58
  110.0 7.2 %reshape.361 = bf16[4,2,4096]{2,1,0:T(2,128)(2,1)S(1)} reshape(bf16[4096,2,2,2]{3,2,1,0:T(2,128)(2,1)} %bitcast.41) | data formatting | bytes 131072
  117.2 6.8 %all_to_all.15 = bf16[4,2,4096]{2,1,0:T(2,128)(2,1)S(1)} all-to-all(bf16[4,2,4096]{2,1,0:T(2,128)(2,1)S(1)} %reshape.361), channel_id=1, replica_groups=mesh['stn'=64,'chan'=4] {'chan'}, dimensions={0} | all-to-all | bytes 131072 | tf_op jit(solution)/shard_map/all_to_all | solution.py:90
  123.9 10.0 %reshape.362 = bf16[4096,2,2,2]{3,2,1,0:T(2,128)(2,1)} reshape(bf16[4,2,4096]{2,1,0:T(2,128)(2,1)S(1)} %all_to_all.15) | data formatting | bytes 131072
  133.9 9.7 %copy.47 = bf16[2,4,1024,2,2]{2,1,4,3,0:T(4,128)(2,1)S(1)} copy(bf16[2,4,1024,2,2]{4,3,0,2,1:T(2,128)(2,1)} %bitcast.42) | data formatting | bytes 131072 | tf_op jit(solution)/shard_map/all_to_all | solution.py:90
  145.7 0.7 select_reduce_fusion
  149.3 125.9 %all-gather.2.cloned.1.call-done = bf16[512,1024,4]{1,2,0:T(4,128)(2,1)} async-done(((bf16[8,1024,4]{1,2,0:T(4,128)(2,1)}), bf16[512,1024,4]{1,2,0:T(4,128)(2,1)}) %all-gather.2.cloned.1.call-update) | async-done | bytes 4194320 | tf_op jit(solution)/shard_map/all_gather | solution.py:101
  275.2 10.1 %copy.41 = bf16[512,1024,4]{0,2,1:T(4,128)(2,1)} copy(bf16[512,1024,4]{1,2,0:T(4,128)(2,1)} %all-gather.2.cloned.1.call-done) | data formatting | bytes 8388608 | tf_op jit(solution)/shard_map/all_gather | solution.py:101
  285.3 7.7 %slice_negate_fusion = (bf16[512,1024,2]{0,2,1:T(2,128)(2,1)S(1)}, bf16[512,1024,2]{0,2,1:T(2,128)(2,1)S(1)}) fusion(bf16[512,1024,4]{0,2,1:T(4,128)(2,1)} %copy.41), kind=kLoop, calls=%fused_computation.30 | loop fusion | flops 1048576 | bytes 8388608 | tf_op jit(solution)/shard_map/neg | solution.py:63
  293.1 13.0 %fusion.13 = f32[1024,8,1024]{2,1,0:T(8,128)} fusion(bf16[8,1024,4]{0,2,1:T(4,128)(2,1)S(1)} %copy.42, bf16[512,1024,2]{0,2,1:T(2,128)(2,1)S(1)} %get-tuple-element.19, bf16[512,1024,2]{0,2,1:T(2,128)(2,1)S(1)} %get-tuple-element.18, bf16[512,1024,4]{0,2,1:T(4,128)(2,1)S(1)} %copy-done), kind=kOutput, calls=%fused_computation.19 | convolution fusion | flops 92274688 | bytes 42008576 | tf_op jit(solution)/shard_map/dot_general | solution.py:65
  306.1 32.2 %copy.43 = f32[1024,8,2,512]{0,3,2,1:T(8,128)} copy(f32[1024,8,2,512]{3,1,2,0:T(8,128)} %bitcast.40) | data formatting | bytes 67108864 | tf_op jit(solution)/shard_map/reshape | solution.py:69
  338.3 13.4 %fusion = bf16[8,2,1024,64,8]{2,4,3,1,0:T(8,128)(2,1)S(1)} fusion(f32[1024,8,2,512]{0,3,2,1:T(8,128)} %copy.43, f32[512]{0:T(512)S(1)} %mul.838), kind=kLoop, calls=%fused_computation.2 | loop fusion | flops 16777216 | bytes 50333696 | tf_op jit(solution)/shard_map/reshape | solution.py:103
  351.7 7.0 %copy.44 = bf16[8,2,1024,64,8]{2,4,1,0,3:T(8,128)(2,1)} copy(bf16[8,2,1024,64,8]{2,4,3,1,0:T(8,128)(2,1)S(1)} %fusion) | data formatting | bytes 33554432 | tf_op jit(solution)/shard_map/reshape | solution.py:103
  358.7 10.9 %gather_fusion = bf16[33,8,2,1024,8]{3,4,2,1,0:T(8,128)(2,1)} fusion(bf16[8,2,1024,64,8]{2,4,1,0,3:T(8,128)(2,1)} %copy.44, s32[1024]{0:T(1024)S(1)} %pad_clamp_fusion), kind=kCustom, calls=%fused_computation | custom fusion | bytes 17301636 | tf_op jit(solution)/shard_map/jit(_take)/gather | solution.py:104
  369.6 10.3 %fusion.9 = bf16[8,2,1024,264]{2,3,1,0:T(8,128)(2,1)} fusion(pred[264]{0:T(512)(128)(4,1)S(1)} %copy-done.2, pred[264]{0:T(512)(128)(4,1)S(1)} %copy-done.3, bf16[33,8,2,1024,8]{3,4,2,1,0:T(8,128)(2,1)} %gather_fusion), kind=kLoop, calls=%fused_computation.15 | loop fusion | flops 8650752 | bytes 17302032 | tf_op jit(solution)/shard_map/jit(_where)/select_n | solution.py:105
  (34 shorter events, 5.4 us)
Async XLA Ops:
  6.5 71.9 %copy-start.1 = (bf16[2,17,2,8192]{3,2,1,0:T(2,128)(2,1)S(1)}, bf16[2,17,2,8192]{3,2,1,0:T(2,128)(2,1)}, u32[]{:S(2)}) copy-start(bf16[2,17,2,8192]{3,2,1,0:T(2,128)(2,1)} %param.2) | copy-start | bytes 3342340
  6.5 268.7 %all-gather.2.cloned.1.call-start = ((), (), s32[]{:S(2)}) async-start(), calls=%async_computation.1 | async-start | bytes 4259840 | tf_op jit(solution)/shard_map/all_gather | solution.py:101
  285.3 7.8 %copy-start = (bf16[512,1024,4]{0,2,1:T(4,128)(2,1)S(1)}, bf16[512,1024,4]{0,2,1:T(4,128)(2,1)}, u32[]{:S(2)}) copy-start(bf16[512,1024,4]{0,2,1:T(4,128)(2,1)} %copy.41) | copy-start | bytes 12582916
  358.7 10.9 %copy-start.2 = (pred[264]{0:T(512)(128)(4,1)S(1)}, pred[264]{0:T(512)(128)(4,1)}, u32[]{:S(2)}) copy-start(pred[264]{0:T(512)(128)(4,1)} %broadcast_in_dim.82) | copy-start | bytes 796
  358.7 10.9 %copy-start.3 = (pred[264]{0:T(512)(128)(4,1)S(1)}, pred[264]{0:T(512)(128)(4,1)}, u32[]{:S(2)}) copy-start(pred[264]{0:T(512)(128)(4,1)} %broadcast_in_dim.77) | copy-start | bytes 796
Sparse Core Ops, SparseCore 0:
  144.6 130.5 all-gather.1
where the time goes:
time: 388 us; the launch traced here: 387 us
  waiting for transfers between devices  126 us (32%)
  other arithmetic  117 us (30%)
  local copies, waits for them, and re-layouts  96.8 us (25%)
  matrix products  26.7 us (7%)
  between operations  13.6 us (4%)
  blocking collectives  6.77 us (2%)
    all_gather x1, waiting for transfers between devices, per_device(): lax.all_gather(own, 'stn', axis=0, tiled=True)  126 us
    convert_element_type x1, other arithmetic, twiddles(): sines = jnp.sin(phase).astype(jnp.bfloat16)  35 us
    neg x1, other arithmetic, twiddles(): upper = jnp.concatenate([cosines, -sines], axis=1)  32.4 us
    reshape x1, local copies, waits for them, and re-layouts, correlate(): product = product.reshape(product.shape[0], product.shape[1], 2, rows)  32.2 us
    unnamed x12, local copies, waits for them, and re-layouts  18.6 us
    dot_general x1, matrix products, channelise(): jnp.dot(lhs, table, preferred_element_type=jnp.float32)  13.7 us
    reshape x1, other arithmetic, per_device(): whole = whole.reshape(group_in, 2, CH_WIN, n_stn, group_in)  13.4 us
    dot_general x1, matrix products, correlate(): lax.dot_general(own, rhs, (((2,), (2,)), ((1,), (1,))), preferred_element...  13 us
  transfers between devices with their start and end apart: 1, of which 1 were waited for; matrix products, arithmetic and copies ran while one was open for 1% of the time, Pallas kernels for 0%

commit v1 on v0

--- a/solution.py
+++ b/solution.py
@@ -87,7 +87,10 @@
     frames = samples.shape[1] - TAPS + 1
     cos_rot, sin_rot = rotations(ch_tot, DFT_BLOCK)
     spectrum = channelise(samples, taps_table(), twiddles(DFT_BLOCK), cos_rot, sin_rot, ch_tot)
-    local = lax.all_to_all(spectrum, "chan", split_axis=1, concat_axis=0, tiled=True)
+    local = jnp.concatenate(
+        lax.all_to_all(jnp.stack(jnp.split(spectrum, lax.axis_size("chan"), axis=1)), "chan", 0, 0),
+        axis=0,
+    )
     group_in = local.shape[0]
     own = local.reshape(group_in, CH_WIN, 2 * frames)
     keep_slots = n_stn // 2 + 1

time: 388 us -> 356 us (0.918)
  local copies, waits for them, and re-layouts: 96.8 us -> 66 us
    unnamed x12 -> x10, local copies, waits for them, and re-layouts: 18.6 us -> 1.39 us
    all_to_all x2 -> x0, local copies, waits for them, and re-layouts: 9.8 us -> none  [per_device(): lax.all_to_all(spectrum, 'chan', split_axis=1, concat_axis=0, tiled=True)]
    reshape x1, local copies, waits for them, and re-layouts: 4.81 us -> 0.02 us  [channelise(): return spectrum.reshape(count, ch_tot, 2, frames)]
  transfers between devices with their start and end apart: 1 -> 1, of which waited for: 1 -> 1; matrix products, arithmetic and copies ran while one was open for 1% -> 2% of each run, Pallas kernels for 0% -> 0%
where the time goes in v1:
time: 356 us; the launch traced here: 355 us
  waiting for transfers between devices  125 us (35%)
  other arithmetic  117 us (33%)
  local copies, waits for them, and re-layouts  66 us (19%)
  matrix products  26.7 us (8%)
  between operations  13.6 us (4%)
  blocking collectives  6.77 us (2%)
    all_gather x1, waiting for transfers between devices, per_device(): lax.all_gather(own, 'stn', axis=0, tiled=True)  125 us
    convert_element_type x1, other arithmetic, twiddles(): sines = jnp.sin(phase).astype(jnp.bfloat16)  35 us
    neg x1, other arithmetic, twiddles(): upper = jnp.concatenate([cosines, -sines], axis=1)  32.4 us
    reshape x1, local copies, waits for them, and re-layouts, correlate(): product = product.reshape(product.shape[0], product.shape[1], 2, rows)  32.3 us
    dot_general x1, matrix products, channelise(): jnp.dot(lhs, table, preferred_element_type=jnp.float32)  13.7 us
    reshape x1, other arithmetic, per_device(): whole = whole.reshape(group_in, 2, CH_WIN, n_stn, group_in)  13.4 us
    dot_general x1, matrix products, correlate(): lax.dot_general(own, rhs, (((2,), (2,)), ((1,), (1,))), preferred_element...  13 us
    gather x1, local copies, waits for them, and re-layouts, per_device(): picked = jnp.take(whole, slot_column, axis=3)  10.9 us
  transfers between devices with their start and end apart: 1, of which 1 were waited for; matrix products, arithmetic and copies ran while one was open for 2% of the time, Pallas kernels for 0%

profile of v1, /device:TPU:2, one launch (start us, length us, event | category | flops | bytes accessed | tf_op | source)
XLA Modules:
  0.0 355.0 jit_solution(14517508592413898480)
XLA Ops:
  6.5 2.4 fusion.33
  8.9 2.1 fusion.45
  11.0 35.0 %sine_convert_fusion = (bf16[8192,256]{1,0:T(8,128)(2,1)}, bf16[8192,256]{1,0:T(8,128)(2,1)}) fusion(), kind=kLoop, calls=%fused_computation.25 | loop fusion | flops 33554432 | bytes 8388608 | tf_op jit(solution)/shard_map/convert_element_type | solution.py:25
  46.0 32.4 %fusion.22 = bf16[8192,256]{1,0:T(8,128)(2,1)} fusion(), kind=kLoop, calls=%fused_computation.34 | loop fusion | flops 37748736 | bytes 4194304 | tf_op jit(solution)/shard_map/neg | solution.py:26
  78.4 2.1 multiply_add_fusion.1
  81.0 4.4 %add_convert_fusion = (bf16[16,2,2,1,8192]{4,3,2,1,0:T(2,128)(2,1)S(1)}, bf16[16,2,2,1,8192]{4,3,2,1,0:T(2,128)(2,1)S(1)}) fusion(f32[16,8192]{1,0:T(8,128)S(1)} %get-tuple-element.46, f32[2,2,8192]{2,1,0:T(2,128)S(1)} %get-tuple-element.44, f32[16,8192]{1,0:T(8,128)S(1)} %get-tuple-element.47, f32[2,2,8192]{2,1,0:T(2,128)S(1)} %get-tuple-element.45), kind=kLoop, calls=%fused_computation.33 | loop fusion | flops 4194304 | bytes 3407872 | tf_op jit(solution)/shard_map/convert
  85.4 4.8 %pad_maximum_fusion = bf16[16,2,2,2,8192]{4,3,2,1,0:T(2,128)(2,1)S(1)} fusion(bf16[16,2,2,1,8192]{4,3,2,1,0:T(2,128)(2,1)S(1)} %get-tuple-element.21, bf16[16,2,2,1,8192]{4,3,2,1,0:T(2,128)(2,1)S(1)} %get-tuple-element.20), kind=kLoop, calls=%fused_computation.31 | loop fusion | flops 4194304 | bytes 4194304 | tf_op jit(solution)/shard_map/stack | solution.py:53
  90.2 1.2 copy.50
  91.4 13.7 %fusion.26 = bf16[64,512]{1,0:T(8,128)(2,1)S(1)} fusion(bf16[64,16384]{1,0:T(8,128)(2,1)S(1)} %bitcast.49, bf16[8192,256]{1,0:T(8,128)(2,1)} %get-tuple-element.49, bf16[8192,256]{1,0:T(8,128)(2,1)} %get-tuple-element.48, bf16[8192,256]{1,0:T(8,128)(2,1)} %fusion.22), kind=kOutput, calls=%fused_computation.36 | convolution fusion | flops 1140916224 | bytes 14745600 | tf_op jit(solution)/shard_map/dot_general | solution.py:55
  105.4 6.8 %all_to_all.5 = bf16[4,2,1024,2,2]{2,4,3,1,0:T(2,128)(2,1)S(1)} all-to-all(bf16[4,2,1024,2,2]{2,4,3,1,0:T(2,128)(2,1)S(1)} %pad_maximum_fusion.1), channel_id=1, replica_groups=mesh['stn'=64,'chan'=4] {'chan'}, dimensions={0} | all-to-all | bytes 131072 | tf_op jit(solution)/shard_map/all_to_all | solution.py:91
  112.8 0.7 compare_bitcast_fusion
  114.0 0.7 select_reduce_fusion
  114.8 0.7 broadcast_in_dim.82
  116.3 0.7 broadcast_in_dim.77
  117.0 1.6 copy.41
  118.6 124.9 %all-gather.2.cloned.1.call-done = bf16[512,1024,4]{1,2,0:T(4,128)(2,1)} async-done(((bf16[8,1024,4]{1,2,0:T(4,128)(2,1)}), bf16[512,1024,4]{1,2,0:T(4,128)(2,1)}) %all-gather.2.cloned.1.call-update) | async-done | bytes 4194320 | tf_op jit(solution)/shard_map/all_gather | solution.py:104
  243.5 10.1 %copy.40 = bf16[512,1024,4]{0,2,1:T(4,128)(2,1)} copy(bf16[512,1024,4]{1,2,0:T(4,128)(2,1)} %all-gather.2.cloned.1.call-done) | data formatting | bytes 8388608 | tf_op jit(solution)/shard_map/all_gather | solution.py:104
  253.6 7.7 %slice_negate_fusion = (bf16[512,1024,2]{0,2,1:T(2,128)(2,1)S(1)}, bf16[512,1024,2]{0,2,1:T(2,128)(2,1)S(1)}) fusion(bf16[512,1024,4]{0,2,1:T(4,128)(2,1)} %copy.40), kind=kLoop, calls=%fused_computation.30 | loop fusion | flops 1048576 | bytes 8388608 | tf_op jit(solution)/shard_map/neg | solution.py:63
  261.4 13.0 %fusion.13 = f32[1024,8,1024]{2,1,0:T(8,128)} fusion(bf16[8,1024,4]{0,2,1:T(4,128)(2,1)S(1)} %copy.41, bf16[512,1024,2]{0,2,1:T(2,128)(2,1)S(1)} %get-tuple-element.19, bf16[512,1024,2]{0,2,1:T(2,128)(2,1)S(1)} %get-tuple-element.18, bf16[512,1024,4]{0,2,1:T(4,128)(2,1)S(1)} %copy-done), kind=kOutput, calls=%fused_computation.19 | convolution fusion | flops 92274688 | bytes 42008576 | tf_op jit(solution)/shard_map/dot_general | solution.py:65
  274.4 32.3 %copy.42 = f32[1024,8,2,512]{0,3,2,1:T(8,128)} copy(f32[1024,8,2,512]{3,1,2,0:T(8,128)} %bitcast.47) | data formatting | bytes 67108864 | tf_op jit(solution)/shard_map/reshape | solution.py:69
  306.6 13.4 %fusion = bf16[8,2,1024,64,8]{2,4,3,1,0:T(8,128)(2,1)S(1)} fusion(f32[1024,8,2,512]{0,3,2,1:T(8,128)} %copy.42, f32[512]{0:T(512)S(1)} %mul.838), kind=kLoop, calls=%fused_computation.2 | loop fusion | flops 16777216 | bytes 50333696 | tf_op jit(solution)/shard_map/reshape | solution.py:106
  320.0 7.0 %copy.43 = bf16[8,2,1024,64,8]{2,4,1,0,3:T(8,128)(2,1)} copy(bf16[8,2,1024,64,8]{2,4,3,1,0:T(8,128)(2,1)S(1)} %fusion) | data formatting | bytes 33554432 | tf_op jit(solution)/shard_map/reshape | solution.py:106
  327.0 10.9 %gather_fusion = bf16[33,8,2,1024,8]{3,4,2,1,0:T(8,128)(2,1)} fusion(bf16[8,2,1024,64,8]{2,4,1,0,3:T(8,128)(2,1)} %copy.43, s32[1024]{0:T(1024)S(1)} %pad_clamp_fusion), kind=kCustom, calls=%fused_computation | custom fusion | bytes 17301636 | tf_op jit(solution)/shard_map/jit(_take)/gather | solution.py:107
  337.9 10.3 %fusion.9 = bf16[8,2,1024,264]{2,3,1,0:T(8,128)(2,1)} fusion(pred[264]{0:T(512)(128)(4,1)S(1)} %copy-done.2, pred[264]{0:T(512)(128)(4,1)S(1)} %copy-done.3, bf16[33,8,2,1024,8]{3,4,2,1,0:T(8,128)(2,1)} %gather_fusion), kind=kLoop, calls=%fused_computation.15 | loop fusion | flops 8650752 | bytes 17302032 | tf_op jit(solution)/shard_map/jit(_where)/select_n | solution.py:108
  (31 shorter events, 2.7 us)
Async XLA Ops:
  6.5 71.9 %copy-start.1 = (bf16[2,17,2,8192]{3,2,1,0:T(2,128)(2,1)S(1)}, bf16[2,17,2,8192]{3,2,1,0:T(2,128)(2,1)}, u32[]{:S(2)}) copy-start(bf16[2,17,2,8192]{3,2,1,0:T(2,128)(2,1)} %param.2) | copy-start | bytes 3342340
  6.5 237.0 %all-gather.2.cloned.1.call-start = ((), (), s32[]{:S(2)}) async-start(), calls=%async_computation.1 | async-start | bytes 4259840 | tf_op jit(solution)/shard_map/all_gather | solution.py:104
  253.6 7.8 %copy-start = (bf16[512,1024,4]{0,2,1:T(4,128)(2,1)S(1)}, bf16[512,1024,4]{0,2,1:T(4,128)(2,1)}, u32[]{:S(2)}) copy-start(bf16[512,1024,4]{0,2,1:T(4,128)(2,1)} %copy.40) | copy-start | bytes 12582916
  327.0 10.9 %copy-start.2 = (pred[264]{0:T(512)(128)(4,1)S(1)}, pred[264]{0:T(512)(128)(4,1)}, u32[]{:S(2)}) copy-start(pred[264]{0:T(512)(128)(4,1)} %broadcast_in_dim.82) | copy-start | bytes 796
  327.0 10.9 %copy-start.3 = (pred[264]{0:T(512)(128)(4,1)S(1)}, pred[264]{0:T(512)(128)(4,1)}, u32[]{:S(2)}) copy-start(pred[264]{0:T(512)(128)(4,1)} %broadcast_in_dim.77) | copy-start | bytes 796
Sparse Core Ops, SparseCore 0:
  112.9 130.5 all-gather.1
